TPU v7x, 512 devices: a whole 4x4x16 slice. The times are simulated.
512 devices in a mesh: row: 16 (over x, y), col: 32 (over z, core).
Axes of the slice: x: 4, y: 4, z: 16, core: 2. Of those that a mesh axis runs over, the one named last changes fastest.
Arguments:
- species: float32 [512, 256, 2048], P(None, 'col', 'row'), may hold values from -26 to 26, as said below
- start_basis: float32 [512, 256], replicated, may hold values from -6 to 6
Outputs:
- core_fibers: float32 [256, 256, 2048], P('row', 'col')
- basis: float32 [512, 256], replicated
Inputs may be any that keep to these rules, and one draw needn't show every extreme that they name: `species`: entries of the slab.
All inputs are finite; a program needn't handle non-finite values.
Results may differ from a plain program's by a relative error of at most 0.00019.
Values sent between devices are 32-bit elements; how exact they have to be, the bound alone decides.
No kernel may reach another device: no remote copies, remote signals or barrier semaphores. Data moves between devices by JAX's collectives and lax.ppermute only.
A program may use at most 64 MiB of HBM per device.

v0:
```python
import jax
import jax.numpy as jnp
from jax import lax
from jax.sharding import PartitionSpec as P

ITERS = 2


def orthonormalize(applied):
    inner_gram = jnp.dot(
        applied.T, applied, precision=lax.Precision.HIGHEST, preferred_element_type=jnp.float32
    )
    small_lower = jnp.linalg.cholesky(inner_gram)
    return jax.scipy.linalg.solve_triangular(small_lower, applied.T, lower=True).T


def power_steps(tri_lower, start_basis):
    current = start_basis
    for sweep_number in range(ITERS):
        halfway = jnp.dot(
            tri_lower.T,
            current,
            precision=lax.Precision.HIGHEST,
            preferred_element_type=jnp.float32,
        )
        applied = jnp.dot(
            tri_lower, halfway, precision=lax.Precision.HIGHEST, preferred_element_type=jnp.float32
        )
        current = orthonormalize(applied)
    return current


def shards(species, start_basis):
    width_x, cells_z, cells_y = species.shape
    fibers = species.reshape(width_x, cells_z * cells_y)
    local_gram = jnp.dot(
        fibers, fibers.T, precision=lax.Precision.HIGHEST, preferred_element_type=jnp.float32
    )
    gram_sum = lax.psum(local_gram, ("row", "col"))
    basis = power_steps(jnp.linalg.cholesky(gram_sum), start_basis)
    core_flat = jnp.dot(
        basis.T, fibers, precision=lax.Precision.HIGHEST, preferred_element_type=jnp.float32
    )
    core_block = core_flat.reshape(basis.shape[1], cells_z, cells_y)
    core_fibers = lax.all_to_all(core_block, "row", split_axis=0, concat_axis=2, tiled=True)
    return (core_fibers, basis)


def solution(mesh):
    in_specs = (P(None, "col", "row"), P())
    out_specs = (P("row", "col", None), P())
    return jax.shard_map(shards, mesh=mesh, in_specs=in_specs, out_specs=out_specs, check_vma=False)
```

profile of v0, /device:TPU:1, one launch (start us, length us, event | category | flops | bytes accessed | tf_op | source)
XLA Modules:
  0.0 744.2 jit_solution(14799633142379794219)
XLA Ops:
  7.2 7.1 fusion.2
  14.4 2.1 copy.41
  16.4 2.3 copy.25
  18.8 468.0 %all-reduce.4.cloned.1.call-done = f32[512,512]{0,1:T(8,128)} async-done(((f32[512,512]{0,1:T(8,128)}), f32[512,512]{0,1:T(8,128)}) %all-reduce.4.cloned.1.call-update) | async-done | bytes 1048592 | tf_op jit(solution)/shard_map/psum | solution.py:39
  486.8 1.6 copy.19
  488.4 0.2 fusion.6
  488.7 1.0 copy-done.2
  489.7 11.7 %cholesky.136 = f32[128,128]{1,0:T(8,128)S(1)} custom-call(f32[128,128]{1,0:T(8,128)S(1)} %cholesky.407), custom_call_target="Cholesky" | custom-call | tf_op jit(solution)/shard_map/jit(cholesky)/cholesky | solution.py:40
  501.4 9.8 %custom-call.32 = f32[1,128,128]{1,2,0:T(8,128)S(1)} custom-call(f32[1,128,128]{2,1,0:T(8,128)S(1)} %get-tuple-element.62), custom_call_target="InvertDiagBlocksLowerTriangular" | custom-call | tf_op jit(solution)/shard_map/jit(cholesky)/cholesky | solution.py:40
  511.3 1.2 constant_dynamic-update-slice_fusion.5
  512.6 1.3 convolution_subtract_fusion.2
  513.9 11.7 %cholesky.159 = f32[128,128]{1,0:T(8,128)S(1)} custom-call(f32[128,128]{1,0:T(8,128)S(1)} %cholesky.411), custom_call_target="Cholesky" | custom-call | tf_op jit(solution)/shard_map/jit(cholesky)/cholesky | solution.py:40
  525.6 10.0 %custom-call.33 = f32[1,128,128]{1,2,0:T(8,128)S(1)} custom-call(f32[1,128,128]{2,1,0:T(8,128)S(1)} %get-tuple-element.59), custom_call_target="InvertDiagBlocksLowerTriangular" | custom-call | tf_op jit(solution)/shard_map/jit(cholesky)/cholesky | solution.py:40
  535.6 0.3 convolution_dynamic-update-slice_fusion
  535.8 1.3 convolution_subtract_fusion.3
  537.1 11.7 %cholesky.294 = f32[128,128]{1,0:T(8,128)S(1)} custom-call(f32[128,128]{1,0:T(8,128)S(1)} %cholesky.416), custom_call_target="Cholesky" | custom-call | tf_op jit(solution)/shard_map/jit(cholesky)/cholesky | solution.py:40
  548.9 0.7 compare_reduce_fusion.5
  549.5 9.8 %custom-call.39 = f32[1,128,128]{1,2,0:T(8,128)S(1)} custom-call(f32[1,128,128]{2,1,0:T(8,128)S(1)} %get-tuple-element.56), custom_call_target="InvertDiagBlocksLowerTriangular" | custom-call | tf_op jit(solution)/shard_map/jit(cholesky)/cholesky/custom-call.9 | solution.py:40
  559.6 1.2 convolution_subtract_fusion.6
  560.8 11.7 %cholesky.307 = f32[128,128]{1,0:T(8,128)S(1)} custom-call(f32[128,128]{1,0:T(8,128)S(1)} %convolution_subtract_fusion.6), custom_call_target="Cholesky" | custom-call | tf_op jit(solution)/shard_map/jit(cholesky)/cholesky | solution.py:40
  572.6 0.7 compare_reduce_fusion.4
  573.2 0.6 compare_reduce_fusion.6
  576.4 1.6 fusion.15
  578.0 1.0 fusion.14
  579.0 1.0 fusion.66
  580.2 11.7 %cholesky.357 = f32[128,128]{1,0:T(8,128)S(1)} custom-call(f32[128,128]{1,0:T(8,128)S(1)} %cholesky.420), custom_call_target="Cholesky" | custom-call | tf_op jit(solution)/shard_map/jit(cholesky)/cholesky | solution.py:13
  592.0 0.6 compare_reduce_fusion.3
  592.6 9.8 %custom-call.40 = f32[1,128,128]{1,2,0:T(8,128)S(1)} custom-call(f32[1,128,128]{2,1,0:T(8,128)S(1)} %get-tuple-element.52), custom_call_target="InvertDiagBlocksLowerTriangular" | custom-call | tf_op jit(solution)/shard_map/jit(cholesky)/cholesky/custom-call.9 | solution.py:13
  602.7 0.3 convolution_subtract_fusion.5
  603.0 11.8 %cholesky.367 = f32[128,128]{1,0:T(8,128)S(1)} custom-call(f32[128,128]{1,0:T(8,128)S(1)} %convolution_subtract_fusion.5), custom_call_target="Cholesky" | custom-call | tf_op jit(solution)/shard_map/jit(cholesky)/cholesky | solution.py:13
  614.8 0.6 compare_reduce_fusion.2
  616.9 4.0 while.4
  616.9 0.6 fusion.87
  617.5 1.4 bitcast_dynamic-update-slice_fusion.4
  618.9 0.6 fusion.87
  619.5 1.4 bitcast_dynamic-update-slice_fusion.4
  620.9 19.7 %custom-call.41 = f32[2,128,128]{1,2,0:T(8,128)S(1)} custom-call(f32[2,128,128]{2,1,0:T(8,128)S(1)} %get-tuple-element.19), custom_call_target="InvertDiagBlocksLowerTriangular" | custom-call | tf_op jit(solution)/shard_map/jit(_solve_triangular)/triangular_solve | solution.py:14
  640.6 0.4 fusion.19
  641.0 0.6 convolution_subtract_fusion.1
  641.6 0.4 fusion.33
  642.0 1.2 fusion.7
  643.3 1.0 fusion.13
  644.3 1.0 fusion.67
  645.5 11.7 %cholesky.384 = f32[128,128]{1,0:T(8,128)S(1)} custom-call(f32[128,128]{1,0:T(8,128)S(1)} %cholesky.423), custom_call_target="Cholesky" | custom-call | tf_op jit(solution)/shard_map/jit(cholesky)/cholesky | solution.py:13
  657.2 0.6 compare_reduce_fusion.1
  657.9 9.8 %custom-call.42 = f32[1,128,128]{1,2,0:T(8,128)S(1)} custom-call(f32[1,128,128]{2,1,0:T(8,128)S(1)} %get-tuple-element.48), custom_call_target="InvertDiagBlocksLowerTriangular" | custom-call | tf_op jit(solution)/shard_map/jit(cholesky)/cholesky/custom-call.9 | solution.py:13
  667.9 0.3 convolution_subtract_fusion.4
  668.2 11.9 %cholesky.394 = f32[128,128]{1,0:T(8,128)S(1)} custom-call(f32[128,128]{1,0:T(8,128)S(1)} %convolution_subtract_fusion.4), custom_call_target="Cholesky" | custom-call | tf_op jit(solution)/shard_map/jit(cholesky)/cholesky | solution.py:13
  680.1 0.6 compare_reduce_fusion
  682.1 4.0 while.5
  682.2 0.6 fusion.88
  682.7 1.4 bitcast_dynamic-update-slice_fusion.5
  684.2 0.6 fusion.88
  684.7 1.4 bitcast_dynamic-update-slice_fusion.5
  686.1 19.7 %custom-call.43 = f32[2,128,128]{1,2,0:T(8,128)S(1)} custom-call(f32[2,128,128]{2,1,0:T(8,128)S(1)} %get-tuple-element.20), custom_call_target="InvertDiagBlocksLowerTriangular" | custom-call | tf_op jit(solution)/shard_map/jit(_solve_triangular)/triangular_solve | solution.py:14
  705.8 0.4 fusion.17
  706.2 0.6 convolution_subtract_fusion
  706.8 0.4 fusion.30
  707.3 3.5 fusion.11
  710.8 1.6 copy.26
  712.4 6.2 all-to-all-start
  718.6 1.0 copy.28
  719.6 16.4 %all-to-all-done = f32[256,8,128]{2,1,0:T(8,128)S(1)} async-done(((f32[256,8,128]{2,1,0:T(8,128)}), f32[256,8,128]{2,1,0:T(8,128)S(1)}, u32[]{:S(2)}, u32[]{:S(2)}) %all-to-all-start) | async-done | bytes 1048608 | tf_op jit(solution)/shard_map/all_to_all | solution.py:45
  736.1 1.1 copy.42
  (41 shorter events, 1.7 us)
Async XLA Ops:
  7.2 569.2 %copy-start = (f32[512,256]{1,0:T(8,128)S(1)}, f32[512,256]{1,0:T(8,128)}, u32[]{:S(2)}) copy-start(f32[512,256]{1,0:T(8,128)} %param.8) | copy-start | bytes 1572868
  7.2 479.6 %all-reduce.4.cloned.1.call-start = ((), (), s32[]{:S(2)}) async-start(), calls=%async_computation.1 | async-start | bytes 2097152 | tf_op jit(solution)/shard_map/psum | solution.py:39
  486.8 1.7 copy-start.1
  488.7 1.0 copy-start.2
  712.4 23.7 %all-to-all-start = ((f32[256,8,128]{2,1,0:T(8,128)}), f32[256,8,128]{2,1,0:T(8,128)S(1)}, u32[]{:S(2)}, u32[]{:S(2)}) async-start(f32[256,8,128]{2,1,0:T(8,128)} %copy.26), calls=%async_computation | async-start | bytes 2097152 | tf_op jit(solution)/shard_map/all_to_all | solution.py:45
Sparse Core Ops, SparseCore 0:
  14.5 472.2 all-reduce.3
where the time goes:
time: 749 us; the launch traced here: 744 us
  waiting for transfers between devices  484 us (65%)
  other arithmetic  188 us (25%)
  matrix products  26.7 us (4%)
  between operations  19.8 us (3%)
  local copies, waits for them, and re-layouts  19.1 us (3%)
    psum x1, waiting for transfers between devices, shards(): gram_sum = lax.psum(local_gram, ('row', 'col'))  468 us
    another operation x14, other arithmetic, shards(): basis = power_steps(jnp.linalg.cholesky(gram_sum), start_basis)  78.5 us
    another operation x14, other arithmetic, orthonormalize(): small_lower = jnp.linalg.cholesky(inner_gram)  69.5 us
    another operation x5, other arithmetic, orthonormalize(): jax.scipy.linalg.solve_triangular(small_lower, applied.T, lower=True)  39.4 us
    all_to_all x1, waiting for transfers between devices, shards(): lax.all_to_all(core_block, 'row', split_axis=0, concat_axis=2, tiled=True)  16.4 us
  transfers between devices with their start and end apart: 2, of which 2 were waited for; matrix products, arithmetic and copies ran while one was open for 1% of the time, Pallas kernels for 0%

commit v1 on v0

--- a/solution.py
+++ b/solution.py
@@ -36,7 +36,8 @@
     local_gram = jnp.dot(
         fibers, fibers.T, precision=lax.Precision.HIGHEST, preferred_element_type=jnp.float32
     )
-    gram_sum = lax.psum(local_gram, ("row", "col"))
+    partial = lax.psum(local_gram, "row")
+    gram_sum = lax.psum(partial, "col")
     basis = power_steps(jnp.linalg.cholesky(gram_sum), start_basis)
     core_flat = jnp.dot(
         basis.T, fibers, precision=lax.Precision.HIGHEST, preferred_element_type=jnp.float32

time: 749 us -> 610 us (0.81)
  waiting for transfers between devices: 484 us -> 345 us
    psum x1 -> x2, waiting for transfers between devices: 468 us -> 331 us  [the longest x1 209 us: shards(): gram_sum = lax.psum(partial, 'col')]
  transfers between devices with their start and end apart: 2 -> 3, of which waited for: 2 -> 3; matrix products, arithmetic and copies ran while one was open for 1% -> 1% of each run, Pallas kernels for 0% -> 0%
where the time goes in v1:
time: 610 us; the launch traced here: 605 us
  waiting for transfers between devices  345 us (57%)
  other arithmetic  188 us (31%)
  matrix products  26.7 us (4%)
  between operations  19.8 us (3%)
  local copies, waits for them, and re-layouts  19.1 us (3%)
  starting transfers between devices  6.61 us (1%)
    psum x1, waiting for transfers between devices, shards(): gram_sum = lax.psum(partial, 'col')  209 us
    psum x1, waiting for transfers between devices, shards(): partial = lax.psum(local_gram, 'row')  122 us
    another operation x14, other arithmetic, shards(): basis = power_steps(jnp.linalg.cholesky(gram_sum), start_basis)  78.5 us
    another operation x14, other arithmetic, orthonormalize(): small_lower = jnp.linalg.cholesky(inner_gram)  69.5 us
    another operation x5, other arithmetic, orthonormalize(): jax.scipy.linalg.solve_triangular(small_lower, applied.T, lower=True)  39.4 us
    all_to_all x1, waiting for transfers between devices, shards(): lax.all_to_all(core_block, 'row', split_axis=0, concat_axis=2, tiled=True)  14 us
  transfers between devices with their start and end apart: 3, of which 3 were waited for; matrix products, arithmetic and copies ran while one was open for 1% of the time, Pallas kernels for 0%

profile of v1, /device:TPU:1, one launch (start us, length us, event | category | flops | bytes accessed | tf_op | source)
XLA Modules:
  0.0 604.8 jit_solution(14311546948960078555)
XLA Ops:
  7.2 7.1 %fusion.2 = f32[512,512]{0,1:T(8,128)} fusion(f32[512,8,128]{2,1,0:T(8,128)} %param.7), kind=kOutput, calls=%fused_computation.7 | convolution fusion | flops 3221225472 | bytes 3145728 | tf_op jit(solution)/shard_map/dot_general | solution.py:36
  14.4 121.7 %all-reduce.5.cloned.1.call-done = f32[512,512]{0,1:T(8,128)} async-done(((f32[512,512]{0,1:T(8,128)}), f32[512,512]{0,1:T(8,128)}) %all-reduce.5.cloned.1.call-update) | async-done | bytes 1048592 | tf_op jit(solution)/shard_map/psum | solution.py:39
  136.1 2.1 copy.41
  138.2 2.3 copy.25
  140.5 208.9 %all-reduce.7.cloned.1.call-done = f32[512,512]{0,1:T(8,128)} async-done(((f32[512,512]{0,1:T(8,128)}), f32[512,512]{0,1:T(8,128)}) %all-reduce.7.cloned.1.call-update) | async-done | bytes 1048592 | tf_op jit(solution)/shard_map/psum | solution.py:40
  349.5 1.6 copy.19
  351.4 1.0 copy-done.2
  352.4 11.7 %cholesky.136 = f32[128,128]{1,0:T(8,128)S(1)} custom-call(f32[128,128]{1,0:T(8,128)S(1)} %cholesky.407), custom_call_target="Cholesky" | custom-call | tf_op jit(solution)/shard_map/jit(cholesky)/cholesky | solution.py:41
  364.1 9.8 %custom-call.32 = f32[1,128,128]{1,2,0:T(8,128)S(1)} custom-call(f32[1,128,128]{2,1,0:T(8,128)S(1)} %get-tuple-element.62), custom_call_target="InvertDiagBlocksLowerTriangular" | custom-call | tf_op jit(solution)/shard_map/jit(cholesky)/cholesky | solution.py:41
  374.0 1.2 constant_dynamic-update-slice_fusion.5
  375.3 1.3 convolution_subtract_fusion.2
  376.6 11.7 %cholesky.159 = f32[128,128]{1,0:T(8,128)S(1)} custom-call(f32[128,128]{1,0:T(8,128)S(1)} %cholesky.411), custom_call_target="Cholesky" | custom-call | tf_op jit(solution)/shard_map/jit(cholesky)/cholesky | solution.py:41
  388.3 10.0 %custom-call.33 = f32[1,128,128]{1,2,0:T(8,128)S(1)} custom-call(f32[1,128,128]{2,1,0:T(8,128)S(1)} %get-tuple-element.59), custom_call_target="InvertDiagBlocksLowerTriangular" | custom-call | tf_op jit(solution)/shard_map/jit(cholesky)/cholesky | solution.py:41
  398.3 0.3 convolution_dynamic-update-slice_fusion
  398.6 1.3 convolution_subtract_fusion.3
  399.9 11.7 %cholesky.294 = f32[128,128]{1,0:T(8,128)S(1)} custom-call(f32[128,128]{1,0:T(8,128)S(1)} %cholesky.416), custom_call_target="Cholesky" | custom-call | tf_op jit(solution)/shard_map/jit(cholesky)/cholesky | solution.py:41
  411.6 0.7 compare_reduce_fusion.5
  412.3 9.8 %custom-call.39 = f32[1,128,128]{1,2,0:T(8,128)S(1)} custom-call(f32[1,128,128]{2,1,0:T(8,128)S(1)} %get-tuple-element.56), custom_call_target="InvertDiagBlocksLowerTriangular" | custom-call | tf_op jit(solution)/shard_map/jit(cholesky)/cholesky/custom-call.9 | solution.py:41
  422.3 1.2 convolution_subtract_fusion.6
  423.5 11.7 %cholesky.307 = f32[128,128]{1,0:T(8,128)S(1)} custom-call(f32[128,128]{1,0:T(8,128)S(1)} %convolution_subtract_fusion.6), custom_call_target="Cholesky" | custom-call | tf_op jit(solution)/shard_map/jit(cholesky)/cholesky | solution.py:41
  435.3 0.7 compare_reduce_fusion.4
  435.9 0.6 compare_reduce_fusion.6
  439.1 1.6 fusion.15
  440.7 1.0 fusion.14
  441.7 1.0 fusion.66
  442.9 11.7 %cholesky.357 = f32[128,128]{1,0:T(8,128)S(1)} custom-call(f32[128,128]{1,0:T(8,128)S(1)} %cholesky.420), custom_call_target="Cholesky" | custom-call | tf_op jit(solution)/shard_map/jit(cholesky)/cholesky | solution.py:13
  454.7 0.6 compare_reduce_fusion.3
  455.3 9.8 %custom-call.40 = f32[1,128,128]{1,2,0:T(8,128)S(1)} custom-call(f32[1,128,128]{2,1,0:T(8,128)S(1)} %get-tuple-element.52), custom_call_target="InvertDiagBlocksLowerTriangular" | custom-call | tf_op jit(solution)/shard_map/jit(cholesky)/cholesky/custom-call.9 | solution.py:13
  465.4 0.3 convolution_subtract_fusion.5
  465.7 11.8 %cholesky.367 = f32[128,128]{1,0:T(8,128)S(1)} custom-call(f32[128,128]{1,0:T(8,128)S(1)} %convolution_subtract_fusion.5), custom_call_target="Cholesky" | custom-call | tf_op jit(solution)/shard_map/jit(cholesky)/cholesky | solution.py:13
  477.5 0.6 compare_reduce_fusion.2
  479.6 4.0 while.4
  479.6 0.6 fusion.87
  480.2 1.4 bitcast_dynamic-update-slice_fusion.4
  481.6 0.6 fusion.87
  482.2 1.4 bitcast_dynamic-update-slice_fusion.4
  483.6 19.7 %custom-call.41 = f32[2,128,128]{1,2,0:T(8,128)S(1)} custom-call(f32[2,128,128]{2,1,0:T(8,128)S(1)} %get-tuple-element.19), custom_call_target="InvertDiagBlocksLowerTriangular" | custom-call | tf_op jit(solution)/shard_map/jit(_solve_triangular)/triangular_solve | solution.py:14
  503.3 0.4 fusion.19
  503.7 0.6 convolution_subtract_fusion.1
  504.3 0.4 fusion.33
  504.7 1.2 fusion.7
  506.0 1.0 fusion.13
  507.0 1.0 fusion.67
  508.2 11.7 %cholesky.384 = f32[128,128]{1,0:T(8,128)S(1)} custom-call(f32[128,128]{1,0:T(8,128)S(1)} %cholesky.423), custom_call_target="Cholesky" | custom-call | tf_op jit(solution)/shard_map/jit(cholesky)/cholesky | solution.py:13
  519.9 0.6 compare_reduce_fusion.1
  520.6 9.8 %custom-call.42 = f32[1,128,128]{1,2,0:T(8,128)S(1)} custom-call(f32[1,128,128]{2,1,0:T(8,128)S(1)} %get-tuple-element.48), custom_call_target="InvertDiagBlocksLowerTriangular" | custom-call | tf_op jit(solution)/shard_map/jit(cholesky)/cholesky/custom-call.9 | solution.py:13
  530.6 0.3 convolution_subtract_fusion.4
  530.9 11.9 %cholesky.394 = f32[128,128]{1,0:T(8,128)S(1)} custom-call(f32[128,128]{1,0:T(8,128)S(1)} %convolution_subtract_fusion.4), custom_call_target="Cholesky" | custom-call | tf_op jit(solution)/shard_map/jit(cholesky)/cholesky | solution.py:13
  542.8 0.6 compare_reduce_fusion
  544.8 4.0 while.5
  544.9 0.6 fusion.88
  545.4 1.4 bitcast_dynamic-update-slice_fusion.5
  546.9 0.6 fusion.88
  547.4 1.4 bitcast_dynamic-update-slice_fusion.5
  548.8 19.7 %custom-call.43 = f32[2,128,128]{1,2,0:T(8,128)S(1)} custom-call(f32[2,128,128]{2,1,0:T(8,128)S(1)} %get-tuple-element.20), custom_call_target="InvertDiagBlocksLowerTriangular" | custom-call | tf_op jit(solution)/shard_map/jit(_solve_triangular)/triangular_solve | solution.py:14
  568.5 0.4 fusion.17
  568.9 0.6 convolution_subtract_fusion
  569.5 0.4 fusion.30
  570.0 3.5 fusion.11
  573.5 1.6 copy.26
  575.1 6.5 %all-to-all-start = ((f32[256,8,128]{2,1,0:T(8,128)}), f32[256,8,128]{2,1,0:T(8,128)S(1)}, u32[]{:S(2)}, u32[]{:S(2)}) async-start(f32[256,8,128]{2,1,0:T(8,128)} %copy.26), calls=%async_computation | async-start | bytes 2097152 | tf_op jit(solution)/shard_map/all_to_all | solution.py:46
  581.7 1.0 copy.28
  582.7 14.0 %all-to-all-done = f32[256,8,128]{2,1,0:T(8,128)S(1)} async-done(((f32[256,8,128]{2,1,0:T(8,128)}), f32[256,8,128]{2,1,0:T(8,128)S(1)}, u32[]{:S(2)}, u32[]{:S(2)}) %all-to-all-start) | async-done | bytes 1048608 | tf_op jit(solution)/shard_map/all_to_all | solution.py:46
  596.6 1.1 copy.42
  (44 shorter events, 2.0 us)
Async XLA Ops:
  7.2 431.9 %copy-start = (f32[512,256]{1,0:T(8,128)S(1)}, f32[512,256]{1,0:T(8,128)}, u32[]{:S(2)}) copy-start(f32[512,256]{1,0:T(8,128)} %param.8) | copy-start | bytes 1572868
  7.2 128.9 %all-reduce.5.cloned.1.call-start = ((), (), s32[]{:S(2)}) async-start(), calls=%async_computation.1 | async-start | bytes 2097152 | tf_op jit(solution)/shard_map/psum | solution.py:39
  14.4 335.1 %all-reduce.7.cloned.1.call-start = ((), (), s32[]{:S(2)}) async-start(), calls=%async_computation.2 | async-start | bytes 2097152 | tf_op jit(solution)/shard_map/psum | solution.py:40
  349.5 1.7 copy-start.1
  351.4 1.0 copy-start.2
  575.1 21.5 %all-to-all-start = ((f32[256,8,128]{2,1,0:T(8,128)}), f32[256,8,128]{2,1,0:T(8,128)S(1)}, u32[]{:S(2)}, u32[]{:S(2)}) async-start(f32[256,8,128]{2,1,0:T(8,128)} %copy.26), calls=%async_computation | async-start | bytes 2097152 | tf_op jit(solution)/shard_map/all_to_all | solution.py:46
Sparse Core Ops, SparseCore 0:
  14.5 121.5 all-reduce.4
  138.4 210.9 all-reduce.6
